TPU v7x, 256 devices: a whole 4x4x8 slice. The times are simulated.
256 devices in a mesh: dp: 64 (over z, x, core), expert: 4 (over y).
Axes of the slice: x: 4, y: 4, z: 8, core: 2. Of those that a mesh axis runs over, the one named last changes fastest.
Arguments:
- grads: bfloat16 [64, 1024, 3584], P('expert', 'dp'), may hold values from -60 to 60
- momentum: bfloat16 [64, 1024, 3584], P('expert', 'dp'), may hold values from -60 to 60
- owner: int32 [4, 16], P('expert'), may hold values from 0 to 15, each once within a row
- query_weight: bfloat16 [1536, 12288], P('dp'), may hold values from -6 to 6
- key_weight: bfloat16 [512, 8192], P('dp'), may hold values from -6 to 6
- head_maxima: float32 [256, 64], P(('dp', 'expert')), may hold values from 5 to 400
- clip_flags: int32 [64], replicated, may hold values 0 or 1
Outputs:
- new_momentum: bfloat16 [64, 1024, 3584], P('expert', 'dp')
- update: bfloat16 [64, 1024, 3584], P('expert', 'dp')
- owned_update: bfloat16 [4, 64, 1024, 896], P('expert', 'dp')
- clipped_query: bfloat16 [1536, 12288], P('dp')
- clipped_key: bfloat16 [512, 8192], P('dp')
All inputs are finite; a program needn't handle non-finite values.
Results may differ from a plain program's by a relative error of at most 0.013.
Values may be sent and summed in bfloat16 or wider, within the bound.
A program may use at most 64 MiB of HBM per device.

v0:
```python
import math

import jax
import jax.numpy as jnp
from jax import lax
from jax.sharding import PartitionSpec as P

ITERS = 2
HEADS = 64
QNOPE = 128
QROPE = 64


MOMENTUM_DECAY = 0.95
COEF_A = 3.4445
COEF_B = -4.775
COEF_C = 2.0315
EPSILON = 1e-07
CLIP_TAU = 100.0


def from_partner(value, axis, distance):
    mask = 2**distance
    pairs = [(source, source ^ mask) for source in range(lax.axis_size(axis))]
    return lax.ppermute(value, axis, pairs)


def shards(grads, momentum, owner, query_weight, key_weight, head_maxima, clip_flags):
    mat_count, row_count, full_width = grads.shape
    quarter = full_width // 4
    dp_count = lax.axis_size("dp")
    groups = dp_count // 4
    new_momentum = (
        MOMENTUM_DECAY * momentum.astype(jnp.float32) + grads.astype(jnp.float32)
    ).astype(jnp.bfloat16)
    owners = owner[0]
    group_ids = jnp.arange(groups, dtype=jnp.int32)
    matches = owners[:, None] == group_ids[None, :]
    inverse = jnp.sum(jnp.where(matches, group_ids[:, None], 0), axis=0)
    outgoing = jnp.take(new_momentum.reshape(mat_count, row_count, 4, quarter), inverse, axis=0)
    outgoing = outgoing.transpose(0, 2, 1, 3).reshape(groups * 4, row_count, quarter)
    incoming = lax.all_to_all(outgoing, "dp", split_axis=0, concat_axis=0, tiled=True)
    column_block = incoming.reshape(groups * 4 * row_count, quarter)
    squares = jnp.sum(jnp.square(column_block.astype(jnp.float32)))
    for bit_pos in (0, 1):
        squares = squares + from_partner(squares, "dp", bit_pos)
    column_block = (column_block.astype(jnp.float32) * lax.rsqrt(squares + EPSILON)).astype(
        jnp.bfloat16
    )
    for sweep in range(ITERS):
        gram_sum = jnp.dot(column_block, column_block.T, preferred_element_type=jnp.float32)
        for bit_pos in (0, 1):
            gram_sum = gram_sum + from_partner(gram_sum, "dp", bit_pos)
        gram_full = gram_sum.astype(jnp.bfloat16)
        poly_term = (
            COEF_B * gram_full.astype(jnp.float32)
            + COEF_C * jnp.dot(gram_full, gram_full, preferred_element_type=jnp.float32)
        ).astype(jnp.bfloat16)
        column_block = (
            COEF_A * column_block.astype(jnp.float32)
            + jnp.dot(poly_term, column_block, preferred_element_type=jnp.float32)
        ).astype(jnp.bfloat16)
    update_block = (column_block.astype(jnp.float32) * math.sqrt(full_width)).astype(jnp.bfloat16)
    owned_update = update_block.reshape(1, 1, update_block.shape[0], quarter)
    returned = lax.all_to_all(
        update_block.reshape(groups * 4, row_count, quarter),
        "dp",
        split_axis=0,
        concat_axis=0,
        tiled=True,
    )
    returned = (
        returned.reshape(groups, 4, row_count, quarter)
        .transpose(0, 2, 1, 3)
        .reshape(groups, row_count, full_width)
    )
    update = jnp.take(returned, owners, axis=0)
    local_peak = jnp.max(head_maxima, axis=0)
    peak_values = lax.pmax(local_peak, ("dp", "expert"))
    clip_gamma = jnp.where(clip_flags == 1, jnp.minimum(1.0, CLIP_TAU / peak_values), 1.0)
    clip_root = jnp.sqrt(clip_gamma)
    query_rows = query_weight.shape[0]
    query_heads = query_weight.astype(jnp.float32).reshape(query_rows, HEADS, QNOPE + QROPE)
    scaled = jnp.concatenate(
        [
            query_heads[:, :, :QNOPE] * clip_root[None, :, None],
            query_heads[:, :, QNOPE:] * clip_gamma[None, :, None],
        ],
        axis=2,
    )
    clipped_query = scaled.reshape(query_rows, HEADS * (QNOPE + QROPE)).astype(jnp.bfloat16)
    key_rows = key_weight.shape[0]
    key_heads = (
        key_weight.astype(jnp.float32).reshape(key_rows, HEADS, QNOPE) * clip_root[None, :, None]
    )
    clipped_key = key_heads.reshape(key_rows, HEADS * QNOPE).astype(jnp.bfloat16)
    return (new_momentum, update, owned_update, clipped_query, clipped_key)


def solution(mesh):
    in_specs = (
        P("expert", "dp", None),
        P("expert", "dp", None),
        P("expert", None),
        P("dp", None),
        P("dp", None),
        P(("dp", "expert"), None),
        P(),
    )
    out_specs = (
        P("expert", "dp", None),
        P("expert", "dp", None),
        P("expert", "dp", None, None),
        P("dp", None),
        P("dp", None),
    )
    return jax.shard_map(shards, mesh=mesh, in_specs=in_specs, out_specs=out_specs, check_vma=False)
```

profile of v0, /device:TPU:25, one launch (start us, length us, event | category | flops | bytes accessed | tf_op | source)
XLA Modules:
  0.0 423.2 jit_solution(1554574142197867221)
XLA Ops:
  0.6 0.7 select_reduce_fusion
  1.4 3.9 add_convert_fusion.6
  5.3 3.3 reshape.102
  8.6 3.3 gather_fusion
  11.9 2.4 select_bitcast_fusion
  14.3 0.3 copy.16
  14.6 56.2 %all_to_all.10 = bf16[64,16,896]{2,1,0:T(8,128)(2,1)S(1)} all-to-all(bf16[64,16,896]{2,1,0:T(8,128)(2,1)S(1)} %bitcast.31), channel_id=1, replica_groups=mesh['dp'=64,'expert'=4] {'dp'}, dimensions={0} | all-to-all | bytes 3670016 | tf_op jit(solution)/shard_map/all_to_all | solution.py:42
  70.8 1.5 fusion
  72.4 1.9 collective-permute-start
  74.3 1.0 collective-permute-done
  76.5 2.0 collective-permute-start.1
  78.5 0.6 collective-permute-done.1
  79.8 0.3 fusion.1
  80.1 0.0 copy-start.2
  80.1 2.4 fusion.11
  82.5 1.4 collective-permute-start.2
  83.9 6.8 %collective-permute-done.2 = f32[1024,1024]{1,0:T(8,128)S(1)} collective-permute-done((f32[1024,1024]{1,0:T(8,128)S(1)}, f32[1024,1024]{1,0:T(8,128)S(1)}, u32[]{:S(2)}, u32[]{:S(2)}) %collective-permute-start.2) | collective-permute-done | bytes 4194336 | tf_op jit(solution)/shard_map/ppermute | solution.py:25
  90.6 1.4 add.73
  92.0 1.9 copy-done
  94.0 1.2 collective-permute-start.3
  95.2 90.7 %collective-permute-done.3 = f32[1024,1024]{1,0:T(8,128)} collective-permute-done((f32[1024,1024]{1,0:T(8,128)S(1)}, f32[1024,1024]{1,0:T(8,128)}, u32[]{:S(2)}, u32[]{:S(2)}) %collective-permute-start.3) | collective-permute-done | bytes 4194336 | tf_op jit(solution)/shard_map/ppermute | solution.py:25
  185.9 0.0 copy-done.3
  185.9 14.3 %add_convert_fusion.5 = bf16[1024,896]{1,0:T(8,128)(2,1)} fusion(bf16[1024,896]{1,0:T(8,128)(2,1)S(1)} %bitcast.36, f32[1024,1024]{1,0:T(8,128)} %copy-done, f32[1024,1024]{1,0:T(8,128)} %collective-permute-done.3), kind=kOutput, calls=%fused_computation.12 | convolution fusion | flops 4039639040 | bytes 12058624 | tf_op jit(solution)/shard_map/dot_general | solution.py:61
  200.1 4.4 %fusion.12 = f32[1024,1024]{1,0:T(8,128)S(1)} fusion(bf16[1024,896]{1,0:T(8,128)(2,1)} %add_convert_fusion.5), kind=kOutput, calls=%fused_computation.42 | convolution fusion | flops 1879048192 | bytes 6029312 | tf_op jit(solution)/shard_map/dot_general | solution.py:51
  204.5 0.0 copy-start.8
  204.5 1.3 collective-permute-start.4
  205.8 6.8 %collective-permute-done.4 = f32[1024,1024]{1,0:T(8,128)S(1)} collective-permute-done((f32[1024,1024]{1,0:T(8,128)S(1)}, f32[1024,1024]{1,0:T(8,128)S(1)}, u32[]{:S(2)}, u32[]{:S(2)}) %collective-permute-start.4) | collective-permute-done | bytes 4194336 | tf_op jit(solution)/shard_map/ppermute | solution.py:25
  212.6 1.4 add.77
  214.0 0.0 copy-start.1
  214.0 1.9 copy-done.1
  215.9 1.2 collective-permute-start.5
  217.1 90.7 %collective-permute-done.5 = f32[1024,1024]{1,0:T(8,128)} collective-permute-done((f32[1024,1024]{1,0:T(8,128)S(1)}, f32[1024,1024]{1,0:T(8,128)}, u32[]{:S(2)}, u32[]{:S(2)}) %collective-permute-start.5) | collective-permute-done | bytes 4194336 | tf_op jit(solution)/shard_map/ppermute | solution.py:25
  307.8 14.3 %multiply_convert_fusion = bf16[1024,896]{1,0:T(8,128)(2,1)} fusion(bf16[1024,896]{1,0:T(8,128)(2,1)S(1)} %copy-done.8, f32[1024,1024]{1,0:T(8,128)} %copy-done.1, f32[1024,1024]{1,0:T(8,128)} %collective-permute-done.5), kind=kOutput, calls=%fused_computation.10 | convolution fusion | flops 4042391552 | bytes 12058624 | tf_op jit(solution)/shard_map/dot_general | solution.py:61
  322.1 6.2 %all-to-all-start.1 = ((bf16[64,16,896]{2,1,0:T(8,128)(2,1)}), bf16[64,16,896]{2,1,0:T(8,128)(2,1)S(1)}, u32[]{:S(2)}, u32[]{:S(2)}) async-start(bf16[64,16,896]{2,1,0:T(8,128)(2,1)} %bitcast.33), calls=%async_computation.1 | async-start | bytes 3670016 | tf_op jit(solution)/shard_map/all_to_all | solution.py:65
  328.4 1.8 reshape.111
  330.2 84.9 %pmax.7 = f32[64]{0:T(128)S(1)} all-reduce(f32[64]{0:T(128)S(1)} %bitcast.37), channel_id=1, replica_groups=mesh['dp'=64,'expert'=4] {'dp','expert'}, use_global_device_ids=true, to_apply=%region_2.3 | all-reduce | flops 64 | bytes 512 | tf_op jit(solution)/shard_map/pmax | solution.py:79
  415.0 0.2 fusion.3
  415.2 0.0 copy-start.7
  415.2 0.0 copy-start.4
  415.2 0.2 fusion.2
  415.4 0.2 pad_maximum_fusion
  415.6 1.7 convert_element_type.90
  417.3 0.1 broadcast_bitcast_fusion
  417.4 0.7 multiply_convert_fusion.1
  418.1 0.0 all-to-all-done.1
  418.1 1.5 copy.18
  419.5 2.2 gather_fusion.1
  421.7 1.5 broadcast_select_fusion
  (17 shorter events, 0.1 us)
Async XLA Ops:
  72.4 2.9 collective-permute-start
  76.5 2.6 collective-permute-start.1
  80.1 2.4 copy-start.2
  82.5 8.1 %collective-permute-start.2 = (f32[1024,1024]{1,0:T(8,128)S(1)}, f32[1024,1024]{1,0:T(8,128)S(1)}, u32[]{:S(2)}, u32[]{:S(2)}) collective-permute-start(f32[1024,1024]{1,0:T(8,128)S(1)} %fusion.11), channel_id=1, source_target_pairs={{0,4},{4,0},{8,12},{12,8},{16,20},{20,16},{24,28},{28,24},{32,36},... | collective-permute-start | bytes 12582920 | tf_op jit(solution)/shard_map/ppermute | solution.py:25
  83.9 102.0 %copy-start.3 = (bf16[64,16,896]{2,1,0:T(8,128)(2,1)S(1)}, bf16[64,16,896]{2,1,0:T(8,128)(2,1)}, u32[]{:S(2)}) copy-start(bf16[64,16,896]{2,1,0:T(8,128)(2,1)} %copy-done.2) | copy-start | bytes 5505028
  92.0 1.9 copy-start
  94.0 91.9 %collective-permute-start.3 = (f32[1024,1024]{1,0:T(8,128)S(1)}, f32[1024,1024]{1,0:T(8,128)}, u32[]{:S(2)}, u32[]{:S(2)}) collective-permute-start(f32[1024,1024]{1,0:T(8,128)S(1)} %add.73), channel_id=1, source_target_pairs={{0,8},{4,12},{8,0},{12,4},{16,24},{20,28},{24,16},{28,20},{32,40},... | collective-permute-start | bytes 12582920 | tf_op jit(solution)/shard_map/ppermute | solution.py:25
  204.5 103.3 %copy-start.8 = (bf16[1024,896]{1,0:T(8,128)(2,1)S(1)}, bf16[1024,896]{1,0:T(8,128)(2,1)}, u32[]{:S(2)}) copy-start(bf16[1024,896]{1,0:T(8,128)(2,1)} %add_convert_fusion.5) | copy-start | bytes 5505028
  204.5 8.1 %collective-permute-start.4 = (f32[1024,1024]{1,0:T(8,128)S(1)}, f32[1024,1024]{1,0:T(8,128)S(1)}, u32[]{:S(2)}, u32[]{:S(2)}) collective-permute-start(f32[1024,1024]{1,0:T(8,128)S(1)} %fusion.12), channel_id=1, source_target_pairs={{0,4},{4,0},{8,12},{12,8},{16,20},{20,16},{24,28},{28,24},{32,36},... | collective-permute-start | bytes 12582920 | tf_op jit(solution)/shard_map/ppermute | solution.py:25
  214.0 1.9 copy-start.1
  215.9 91.9 %collective-permute-start.5 = (f32[1024,1024]{1,0:T(8,128)S(1)}, f32[1024,1024]{1,0:T(8,128)}, u32[]{:S(2)}, u32[]{:S(2)}) collective-permute-start(f32[1024,1024]{1,0:T(8,128)S(1)} %add.77), channel_id=1, source_target_pairs={{0,8},{4,12},{8,0},{12,4},{16,24},{20,28},{24,16},{28,20},{32,40},... | collective-permute-start | bytes 12582920 | tf_op jit(solution)/shard_map/ppermute | solution.py:25
  322.1 8.0 %copy-start.6 = (f32[1,64]{1,0:T(1,128)S(1)}, f32[1,64]{1,0:T(1,128)}, u32[]{:S(2)}) copy-start(f32[1,64]{1,0:T(1,128)} %param.12) | copy-start | bytes 772
  322.1 92.9 %copy-start.5 = (s32[64]{0:T(128)S(1)}, s32[64]{0:T(128)}, u32[]{:S(2)}) copy-start(s32[64]{0:T(128)} %param.13) | copy-start | bytes 772
  322.1 95.9 %all-to-all-start.1 = ((bf16[64,16,896]{2,1,0:T(8,128)(2,1)}), bf16[64,16,896]{2,1,0:T(8,128)(2,1)S(1)}, u32[]{:S(2)}, u32[]{:S(2)}) async-start(bf16[64,16,896]{2,1,0:T(8,128)(2,1)} %bitcast.33), calls=%async_computation.1 | async-start | bytes 3670016 | tf_op jit(solution)/shard_map/all_to_all | solution.py:65
  415.2 2.0 copy-start.7
  415.2 2.1 copy-start.4
where the time goes:
time: 425 us; the launch traced here: 423 us
  waiting for transfers between devices  196 us (46%)
  blocking collectives  141 us (33%)
  matrix products  35.3 us (8%)
  local copies, waits for them, and re-layouts  17.9 us (4%)
  starting transfers between devices  15.2 us (4%)
  other arithmetic  14.3 us (3%)
    ppermute x6, waiting for transfers between devices, from_partner(): return lax.ppermute(value, axis, pairs)  196 us
    pmax x1, blocking collectives, shards(): peak_values = lax.pmax(local_peak, ('dp', 'expert'))  84.9 us
    all_to_all x1, blocking collectives, shards(): lax.all_to_all(outgoing, 'dp', split_axis=0, concat_axis=0, tiled=True)  56.2 us
    dot_general x2, matrix products, shards(): jnp.dot(poly_term, column_block, preferred_element_type=jnp.float32)  28.5 us
    ppermute x6, starting transfers between devices, from_partner(): return lax.ppermute(value, axis, pairs)  8.98 us
  transfers between devices with their start and end apart: 7, of which 6 were waited for; matrix products, arithmetic and copies ran while one was open for 1% of the time, Pallas kernels for 0%

commit v1 on v0

v1 whole, which is shorter than its diff:
```python
import functools
import math

import jax
import jax.numpy as jnp
from jax import lax
from jax.experimental import pallas as pl
from jax.experimental.pallas import tpu as pltpu
from jax.sharding import PartitionSpec as P

HEADS = 64
QNOPE = 128
QROPE = 64

MOMENTUM_DECAY = 0.95
COEF_A = 3.4445
COEF_B = -4.775
COEF_C = 2.0315
EPSILON = 1e-07
CLIP_TAU = 100.0

MESH = pl.DeviceIdType.MESH
PLANES = 8
SEATS = 8
ROWS = 16
MATS = 16
PLANE_ROWS = SEATS * ROWS
BLOCK = 2 * PLANE_ROWS
HID = PLANES * PLANE_ROWS
STEPS = HID // BLOCK
DEVICES = PLANES * SEATS
LANES = 128


def wrapped(value):
    return lax.rem(value + 64, 8)


def plane_offset(pair, half):
    return half + (1 - 2 * half) * pair * (pair + 1)


def dot_nn(a, b):
    return jnp.dot(a, b, preferred_element_type=jnp.float32)


def dot_nt(a, b):
    return lax.dot_general(a, b, (((1,), (1,)), ((), ())), preferred_element_type=jnp.float32)


def wait_bytes(ref, sem):
    pltpu.make_async_copy(ref, ref, sem).wait()


def step_kernel(
    experts,
    owner_s, grads_h, momentum_h, query_v, key_v, peaks_v, flags_v,
    new_momentum_h, returned_h, owned_h, query_o, key_o,
    grads_v, momentum_v, staged, new_v, x_own, x_pair, x_next, u_own,
    gram, poly, gram_next,
    part0, part1, part2, part3, far0, far1, far2, far3,
    peak_y, peak_z, peak_s, gamma_v, root_v,
    load_sem, store_sem, in_send, in_recv, pair_send, pair_recv,
    far_send, far_recv, share_send, share_recv, out_send, out_recv,
    peak_send, peak_recv,
):
    parts = (part0, part1, part2, part3)
    fars = (far0, far1, far2, far3)
    me = lax.axis_index("dp")
    y = lax.axis_index("expert")
    z = me // SEATS
    seat = lax.rem(me, SEATS)
    core = lax.rem(me, 2)
    group = me // 4
    width = grads_v.shape[2]
    quarter = width // 4
    pair = me + 1 - 2 * core
    across = me + 2 - 4 * lax.rem(me // 2, 2)

    def columns_of(part):
        return pl.ds(pl.multiple_of(part * quarter, LANES), quarter)

    my_columns = columns_of(lax.rem(me, 4))

    def remote(src, dst, send, recv, where):
        return pltpu.make_async_remote_copy(
            src_ref=src, dst_ref=dst, send_sem=send, recv_sem=recv,
            device_id=where, device_id_type=MESH,
        )

    barrier = pltpu.get_barrier_semaphore()

    def greet(i, carry):
        pl.semaphore_signal(
            barrier, inc=1, device_id={"dp": lax.rem(me + i, DEVICES)}, device_id_type=MESH
        )
        return carry

    lax.fori_loop(1, DEVICES, greet, 0)

    def greet_expert(i, carry):
        pl.semaphore_signal(
            barrier, inc=1, device_id={"expert": lax.rem(y + i, experts)}, device_id_type=MESH
        )
        return carry

    lax.fori_loop(1, experts, greet_expert, 0)

    load_grads = pltpu.make_async_copy(grads_h, grads_v, load_sem.at[0])
    load_momentum = pltpu.make_async_copy(momentum_h, momentum_v, load_sem.at[1])
    load_grads.start()
    load_momentum.start()
    peak_y[y] = jnp.zeros((8, LANES), jnp.float32)
    peak_y[y, :, 0:HEADS] = jnp.broadcast_to(peaks_v[...], (8, HEADS))
    load_grads.wait()
    load_momentum.wait()

    def momentum_of(k):
        return (
            MOMENTUM_DECAY * momentum_v[k].astype(jnp.float32) + grads_v[k].astype(jnp.float32)
        ).astype(jnp.bfloat16)

    def stage(g, carry):
        k = jnp.int32(0)
        for m in range(MATS):
            k = jnp.where(owner_s[0, m] == g, m, k)
        staged[g] = momentum_of(k)
        return carry

    lax.fori_loop(0, MATS, stage, 0)
    pl.semaphore_wait(barrier, DEVICES - 1 + experts - 1)

    def send_peak_y(i, carry):
        remote(
            peak_y.at[y], peak_y.at[y], peak_send.at[0], peak_recv.at[0],
            {"expert": lax.rem(y + i, experts)},
        ).start()
        return carry

    lax.fori_loop(1, experts, send_peak_y, 0)

    def send_rows(i, carry):
        t = i // SEATS
        step = lax.rem(t, STEPS)
        half = lax.rem(t // STEPS + z, 2)
        their_z = wrapped(z - plane_offset(step, half))
        their_seat = lax.rem(seat + lax.rem(i, SEATS), SEATS)
        there = their_z * SEATS + their_seat
        src = staged.at[there // 4, :, columns_of(lax.rem(there, 4))]
        row = (2 * step + half) * PLANE_ROWS + seat * ROWS
        dst = x_own.at[pl.ds(pl.multiple_of(row, ROWS), ROWS)]

        @pl.when(there != me)
        def _():
            remote(src, dst, in_send, in_recv.at[step], {"dp": there}).start()

        @pl.when(there == me)
        def _():
            pltpu.make_async_copy(src, dst, in_recv.at[step]).start()

        return carry

    lax.fori_loop(0, DEVICES, send_rows, 0)

    def new_momentum_step(k, carry):
        new_v[k] = momentum_of(k)
        return carry

    lax.fori_loop(0, MATS, new_momentum_step, 0)
    store_momentum = pltpu.make_async_copy(new_v, new_momentum_h, store_sem.at[0])
    store_momentum.start()

    wait_bytes(peak_y.at[pl.ds(0, experts - 1)], peak_recv.at[0])
    peak_z[z] = jnp.max(peak_y[...], axis=0)

    def send_peak_z(i, carry):
        remote(
            peak_z.at[z], peak_z.at[z], peak_send.at[1], peak_recv.at[1],
            {"dp": lax.rem(z + i, PLANES) * SEATS + seat},
        ).start()
        return carry

    lax.fori_loop(1, PLANES, send_peak_z, 0)

    def rows_of(s):
        return pl.ds(s * BLOCK, BLOCK)

    def mine_of(s, which):
        return pl.ds(pl.multiple_of(which * (s + 1) * LANES, LANES), (s + 1) * LANES)

    pair_copies = []
    far_copies = []
    share_copies = []

    def share(s):
        far_copies[s].wait_recv()
        spot = gram.at[rows_of(s), mine_of(s, core)]
        gram[rows_of(s), mine_of(s, core)] = (
            parts[s][...].astype(jnp.float32) + fars[s][...].astype(jnp.float32)
        ).astype(jnp.bfloat16)
        copy = remote(spot, spot, share_send.at[s], share_recv.at[s], {"dp": pair})
        copy.start()
        share_copies.append(copy)

    def mirror(s):
        share_copies[s].wait_recv()
        for j in range(s):
            gram[rows_of(j), rows_of(s)] = gram[rows_of(s), rows_of(j)].T

    for s in range(STEPS):
        wait_bytes(x_own.at[rows_of(s)], in_recv.at[s])
        copy = remote(
            x_own.at[rows_of(s)], x_pair.at[rows_of(s)], pair_send.at[s], pair_recv.at[s],
            {"dp": pair},
        )
        copy.start()
        pair_copies.append(copy)
        copy.wait_recv()
        parts[s][...] = (
            dot_nt(x_own[rows_of(s), :], x_own[mine_of(s, core), :])
            + dot_nt(x_pair[rows_of(s), :], x_pair[mine_of(s, core), :])
        ).astype(jnp.bfloat16)
        copy = remote(parts[s], fars[s], far_send.at[s], far_recv.at[s], {"dp": across})
        copy.start()
        far_copies.append(copy)
        if s > 0:
            share(s - 1)
        if s > 1:
            mirror(s - 2)
    mirror(STEPS - 2)
    share(STEPS - 1)
    mirror(STEPS - 1)

    diagonal = gram[rows_of(0), rows_of(0)].astype(jnp.float32)
    for s in range(1, STEPS):
        diagonal = diagonal + gram[rows_of(s), rows_of(s)].astype(jnp.float32)
    down = lax.broadcasted_iota(jnp.int32, (BLOCK, BLOCK), 0)
    along = lax.broadcasted_iota(jnp.int32, (BLOCK, BLOCK), 1)
    squares = jnp.sum(jnp.where(down == along, diagonal, 0.0), axis=0, keepdims=True)
    squares = jnp.sum(squares, axis=1, keepdims=True)
    scale = lax.rsqrt(squares + EPSILON)
    scale2 = 1.0 / (squares + EPSILON)

    def block_rows(i):
        return pl.ds(pl.multiple_of(i * BLOCK, BLOCK), BLOCK)

    def poly_step(i, carry):
        rows = block_rows(i)
        product = dot_nn(gram[rows, :], gram[...])
        poly[rows, :] = (
            (COEF_B * scale2) * gram[rows, :].astype(jnp.float32)
            + (COEF_C * scale2 * scale2) * product
        ).astype(jnp.bfloat16)
        return carry

    lax.fori_loop(0, STEPS, poly_step, 0)

    def iterate_step(i, carry):
        rows = block_rows(i)
        x_next[rows, :] = (
            scale
            * (COEF_A * x_own[rows, :].astype(jnp.float32) + dot_nn(poly[rows, :], x_own[...]))
        ).astype(jnp.bfloat16)
        return carry

    lax.fori_loop(0, STEPS, iterate_step, 0)

    def gram_step(i, carry):
        rows = block_rows(i)
        left = scale2 * (
            COEF_A * gram[rows, :].astype(jnp.float32) + dot_nn(poly[rows, :], gram[...])
        )
        gram_next[rows, :] = (
            COEF_A * left + dot_nn(left.astype(jnp.bfloat16), poly[...])
        ).astype(jnp.bfloat16)
        return carry

    lax.fori_loop(0, STEPS, gram_step, 0)

    wait_bytes(peak_z.at[pl.ds(0, PLANES - 1)], peak_recv.at[1])
    peak_s[seat] = jnp.max(peak_z[...], axis=0)

    def send_peak_s(i, carry):
        remote(
            peak_s.at[seat], peak_s.at[seat], peak_send.at[2], peak_recv.at[2],
            {"dp": z * SEATS + lax.rem(seat + i, SEATS)},
        ).start()
        return carry

    lax.fori_loop(1, SEATS, send_peak_s, 0)

    def update_step(i, carry):
        rows = block_rows(i)
        own = gram_next[rows, :]
        term = (
            COEF_B * own.astype(jnp.float32) + COEF_C * dot_nn(own, gram_next[...])
        ).astype(jnp.bfloat16)
        last = (
            COEF_A * x_next[rows, :].astype(jnp.float32) + dot_nn(term, x_next[...])
        ).astype(jnp.bfloat16)
        u_own[rows, :] = (last.astype(jnp.float32) * math.sqrt(width)).astype(jnp.bfloat16)

        def send_update(n, inner):
            half = n // SEATS
            their_z = wrapped(z + plane_offset(i, half))
            their_seat = lax.rem(seat + n, SEATS)
            there = their_z * SEATS + their_seat
            row = (2 * i + half) * PLANE_ROWS + their_seat * ROWS
            src = u_own.at[pl.ds(pl.multiple_of(row, ROWS), ROWS)]
            dst = returned_h.at[group, :, my_columns]

            @pl.when(there != me)
            def _():
                remote(src, dst, out_send, out_recv, {"dp": there}).start()

            @pl.when(there == me)
            def _():
                pltpu.make_async_copy(src, dst, out_recv).start()

            return inner

        lax.fori_loop(0, 2 * SEATS, send_update, 0)

        def store_owned(half, inner):
            src = u_own.at[pl.ds(pl.multiple_of((2 * i + half) * PLANE_ROWS, ROWS), PLANE_ROWS)]
            plane = wrapped(z + plane_offset(i, half))
            dst = owned_h.at[0, 0, pl.ds(pl.multiple_of(plane * PLANE_ROWS, ROWS), PLANE_ROWS)]
            pltpu.make_async_copy(src, dst, store_sem.at[1]).start()
            return inner

        lax.fori_loop(0, 2, store_owned, 0)
        return carry

    lax.fori_loop(0, STEPS, update_step, 0)

    wait_bytes(peak_s.at[pl.ds(0, SEATS - 1)], peak_recv.at[2])
    top = jnp.max(peak_s[...], axis=0)
    head_down = lax.broadcasted_iota(jnp.int32, (HEADS, HEADS), 0)
    head_along = lax.broadcasted_iota(jnp.int32, (HEADS, HEADS), 1)
    same = head_down == head_along
    peak = jnp.max(
        jnp.where(same, jnp.broadcast_to(top[0:1, 0:HEADS], (HEADS, HEADS)), 0.0),
        axis=1, keepdims=True,
    )
    flag = jnp.max(
        jnp.where(
            same, jnp.broadcast_to(flags_v[...].astype(jnp.float32), (HEADS, HEADS)), 0.0
        ),
        axis=1, keepdims=True,
    )
    peak = jnp.broadcast_to(peak, (HEADS, LANES))
    flag = jnp.broadcast_to(flag, (HEADS, LANES))
    gamma = jnp.where(flag == 1.0, jnp.minimum(1.0, CLIP_TAU / peak), 1.0)
    gamma_v[...] = gamma
    root_v[...] = jnp.sqrt(gamma)
    low = lax.broadcasted_iota(jnp.int32, (1, LANES), 1) < LANES // 2

    def clip_step(j, carry):
        root0 = root_v[pl.ds(2 * j, 1), :]
        root1 = root_v[pl.ds(2 * j + 1, 1), :]
        gamma0 = gamma_v[pl.ds(2 * j, 1), :]
        gamma1 = gamma_v[pl.ds(2 * j + 1, 1), :]
        scales = (root0, jnp.where(low, gamma0, root1), jnp.where(low, root1, gamma1))
        for n, factor in enumerate(scales):
            lanes = pl.ds(pl.multiple_of((3 * j + n) * LANES, LANES), LANES)
            query_o[:, lanes] = (query_v[:, lanes].astype(jnp.float32) * factor).astype(
                jnp.bfloat16
            )
        for n, factor in enumerate((root0, root1)):
            lanes = pl.ds(pl.multiple_of((2 * j + n) * LANES, LANES), LANES)
            key_o[:, lanes] = (key_v[:, lanes].astype(jnp.float32) * factor).astype(jnp.bfloat16)
        return carry

    lax.fori_loop(0, HEADS // 2, clip_step, 0)

    store_momentum.wait()
    wait_bytes(peak_y.at[pl.ds(0, experts - 1)], peak_send.at[0])
    wait_bytes(peak_z.at[pl.ds(0, PLANES - 1)], peak_send.at[1])
    wait_bytes(peak_s.at[pl.ds(0, SEATS - 1)], peak_send.at[2])
    for copy in pair_copies + far_copies + share_copies:
        copy.wait_send()
    wait_bytes(x_own.at[pl.ds(0, HID - ROWS)], in_send)
    wait_bytes(u_own.at[pl.ds(0, HID - ROWS)], out_send)
    wait_bytes(u_own, store_sem.at[1])
    wait_bytes(returned_h, out_recv)


def pick_kernel(owner_s, returned_h, update_h, sem):
    copies = [
        pltpu.make_async_copy(returned_h.at[owner_s[0, k]], update_h.at[k], sem.at[k])
        for k in range(MATS)
    ]
    for copy in copies:
        copy.start()
    for copy in copies:
        copy.wait()


def shards(experts, grads, momentum, owner, query_weight, key_weight, head_maxima, clip_flags):
    mats, rows, width = grads.shape
    quarter = width // 4
    smem = pl.BlockSpec(memory_space=pltpu.SMEM)
    vmem = pl.BlockSpec(memory_space=pltpu.VMEM)
    anywhere = pl.BlockSpec(memory_space=pl.ANY)
    bf16 = jnp.bfloat16
    shard = jax.ShapeDtypeStruct((mats, rows, width), bf16)
    block = pltpu.VMEM((mats, rows, width), bf16)
    half = pltpu.VMEM((HID, quarter), bf16)
    square = pltpu.VMEM((HID, HID), bf16)
    lanes = [pltpu.VMEM((BLOCK, (s + 1) * LANES), bf16) for s in range(STEPS)]
    dma = pltpu.SemaphoreType.DMA
    new_momentum, returned, owned, query, key = pl.pallas_call(
        functools.partial(step_kernel, experts),
        out_shape=(
            shard,
            shard,
            jax.ShapeDtypeStruct((1, 1, HID, quarter), bf16),
            jax.ShapeDtypeStruct(query_weight.shape, bf16),
            jax.ShapeDtypeStruct(key_weight.shape, bf16),
        ),
        in_specs=[smem, anywhere, anywhere, vmem, vmem, vmem, vmem],
        out_specs=(anywhere, anywhere, anywhere, vmem, vmem),
        scratch_shapes=[
            block, block, block, block, half, half, half, half, square, square, square,
            *lanes, *lanes,
            pltpu.VMEM((experts, 8, LANES), jnp.float32),
            pltpu.VMEM((PLANES, 8, LANES), jnp.float32),
            pltpu.VMEM((SEATS, 8, LANES), jnp.float32),
            pltpu.VMEM((HEADS, LANES), jnp.float32),
            pltpu.VMEM((HEADS, LANES), jnp.float32),
            dma((2,)), dma((2,)), dma, dma((STEPS,)), dma((STEPS,)), dma((STEPS,)),
            dma((STEPS,)), dma((STEPS,)), dma((STEPS,)), dma((STEPS,)), dma, dma,
            dma((3,)), dma((3,)),
        ],
        compiler_params=pltpu.CompilerParams(
            collective_id=0, has_side_effects=True, vmem_limit_bytes=48 * 1024 * 1024
        ),
        name="muon_step",
    )(
        owner, grads, momentum, query_weight, key_weight, head_maxima,
        clip_flags.reshape(1, HEADS),
    )
    update = pl.pallas_call(
        pick_kernel,
        out_shape=shard,
        in_specs=[smem, anywhere],
        out_specs=anywhere,
        scratch_shapes=[dma((MATS,))],
        name="pick_rows",
    )(owner, returned)
    return (new_momentum, update, owned, query, key)


def solution(mesh):
    in_specs = (
        P("expert", "dp", None),
        P("expert", "dp", None),
        P("expert", None),
        P("dp", None),
        P("dp", None),
        P(("dp", "expert"), None),
        P(),
    )
    out_specs = (
        P("expert", "dp", None),
        P("expert", "dp", None),
        P("expert", "dp", None, None),
        P("dp", None),
        P("dp", None),
    )
    return jax.shard_map(
        functools.partial(shards, mesh.shape["expert"]),
        mesh=mesh, in_specs=in_specs, out_specs=out_specs, check_vma=False,
    )
```

time: 425 us -> 193 us (0.45)
  waiting for transfers between devices: 196 us -> 0 us
  Pallas kernels: 0 us -> 182 us
  blocking collectives: 141 us -> 0 us
  matrix products: 35.3 us -> 0 us
  starting transfers between devices: 15.2 us -> 0 us
  other arithmetic: 14.3 us -> 0 us
  local copies, waits for them, and re-layouts: 17.9 us -> 10 us
    ppermute x6 -> x0, waiting for transfers between devices: 196 us -> none  [from_partner(): return lax.ppermute(value, axis, pairs)]
    pallas_call x0 -> x2, Pallas kernels: none -> 182 us  [the longest x1 124 us: shards(): pl.pallas_call(functools.partial(step_kernel, experts), out_shape=(shard,...]
    pmax x1 -> x0, blocking collectives: 84.9 us -> none  [shards(): peak_values = lax.pmax(local_peak, ('dp', 'expert'))]
    all_to_all x1 -> x0, blocking collectives: 56.2 us -> none  [shards(): lax.all_to_all(outgoing, 'dp', split_axis=0, concat_axis=0, tiled=True)]
    dot_general x4 -> x0, matrix products: 35.3 us -> none  [the longest x2 28.5 us: shards(): jnp.dot(poly_term, column_block, preferred_element_type=jnp.float32)]
    ppermute x6 -> x0, starting transfers between devices: 8.98 us -> none  [from_partner(): return lax.ppermute(value, axis, pairs)]
    reshape x3 -> x0, local copies, waits for them, and re-layouts: 6.57 us -> none  [the longest x1 3.31 us: shards(): new_momentum.reshape(mat_count, row_count, 4, quarter)]
    all_to_all x1 -> x0, starting transfers between devices: 6.22 us -> none  [shards(): lax.all_to_all(update_block.reshape(groups * 4, row_count, quarter), 'dp'...]
  transfers between devices with their start and end apart: 7 -> 0, of which waited for: 6 -> 0; matrix products, arithmetic and copies ran while one was open for 1% -> 0% of each run, Pallas kernels for 0% -> 0%
where the time goes in v1:
time: 193 us; the launch traced here: 192 us
  Pallas kernels  182 us (94%)
  local copies, waits for them, and re-layouts  10 us (5%)
    pallas_call x1, Pallas kernels, shards(): pl.pallas_call(functools.partial(step_kernel, experts), out_shape=(shard,...  124 us
    pallas_call x1, Pallas kernels, shards(): pl.pallas_call(pick_kernel, out_shape=shard, in_specs=[smem, anywhere], o...  57.5 us
    unnamed x18, local copies, waits for them, and re-layouts  10 us

profile of v1, /device:TPU:25, one launch (start us, length us, event | category | flops | bytes accessed | tf_op | source)
XLA Modules:
  0.0 192.3 jit_solution(6300042171393453939)
XLA Ops:
  0.6 0.0 copy-start.1
  0.6 1.1 copy-done.1
  1.7 0.0 copy-start.2
  1.7 0.9 copy-done.2
  2.6 0.0 copy-start.3
  2.6 0.7 copy-done.3
  3.3 0.0 copy-start.4
  3.3 0.7 copy-done.4
  3.9 0.0 copy-start.5
  3.9 0.7 copy-done.5
  4.6 124.1 %muon_step.1 = (bf16[16,16,3584]{2,1,0:T(8,128)(2,1)S(1)}, bf16[16,16,3584]{2,1,0:T(8,128)(2,1)S(1)}, bf16[1,1,1024,896]{3,2,1,0:T(8,128)(2,1)}, bf16[24,12288]{1,0:T(8,128)(2,1)S(1)}, bf16[8,8192]{1,0:T(8,128)(2,1)S(1)}) custom-call(s32[1,16]{1,0:T(1,128)S(1)} %copy-done.3, bf16[16,16,3584]{2,1,0:T(8,128)(2,1)} %grads_h.1, ...), custom_call_target="tpu_custom_call" | custom-call | tf_op jit(solution)/shard_map/muon_step/pallas_call | solution.py:412
  128.7 0.0 copy-start
  128.7 1.2 copy-done
  129.9 57.5 %pick_rows.1 = bf16[16,16,3584]{2,1,0:T(8,128)(2,1)} custom-call(s32[1,16]{1,0:T(1,128)} %owner_s.3, bf16[16,16,3584]{2,1,0:T(8,128)(2,1)} %copy-done), custom_call_target="tpu_custom_call" | custom-call | tf_op jit(solution)/shard_map/pick_rows/pallas_call | solution.py:443
  187.4 0.0 copy-start.6
  187.4 1.2 copy.16
  188.7 0.9 copy-done.6
  189.6 1.2 copy.17
  190.8 0.8 copy.18
  191.6 0.7 copy.19
Async XLA Ops:
  0.6 1.1 copy-start.1
  1.7 0.9 copy-start.2
  2.6 0.7 copy-start.3
  3.3 0.7 copy-start.4
  3.9 0.7 copy-start.5
  128.7 1.2 copy-start
  187.4 2.2 %copy-start.6 = (bf16[1,1,1024,896]{3,2,1,0:T(8,128)(2,1)S(1)}, bf16[1,1,1024,896]{3,2,1,0:T(8,128)(2,1)}, u32[]{:S(2)}) copy-start(bf16[1,1,1024,896]{3,2,1,0:T(8,128)(2,1)} %get-tuple-element.22) | copy-start | bytes 5505028

commit v2 on v1

v2 whole, which is shorter than its diff:
```python
import functools
import math

import jax
import jax.numpy as jnp
from jax import lax
from jax.experimental import pallas as pl
from jax.experimental.pallas import tpu as pltpu
from jax.sharding import PartitionSpec as P

HEADS = 64
QNOPE = 128
QROPE = 64

MOMENTUM_DECAY = 0.95
COEF_A = 3.4445
COEF_B = -4.775
COEF_C = 2.0315
EPSILON = 1e-07
CLIP_TAU = 100.0

MESH = pl.DeviceIdType.MESH
PLANES = 8
SEATS = 8
ROWS = 16
MATS = 16
PLANE_ROWS = SEATS * ROWS
BLOCK = 2 * PLANE_ROWS
HID = PLANES * PLANE_ROWS
DEVICES = PLANES * SEATS
LANES = 128

OFFSETS = (3, -3, 2, -2, 1, -1, 0, 4)
LOOK = 2
STEP_SLOTS = ((0, 1), (2, 3), (4, 5), (6,), (7,))
STEPS = len(STEP_SLOTS)
BLOCKS = HID // BLOCK


def wrapped(value):
    return lax.rem(value + 64, 8)


def step_extent(s):
    first = STEP_SLOTS[s][0] * PLANE_ROWS
    count = len(STEP_SLOTS[s]) * PLANE_ROWS
    return first, count, first + count


def part_shape(s):
    _, count, columns = step_extent(s)
    return (count, columns // 2) if columns % BLOCK == 0 and count == BLOCK else (count // 2, columns)


def dot_nn(a, b):
    return jnp.dot(a, b, preferred_element_type=jnp.float32)


def dot_nt(a, b):
    return lax.dot_general(a, b, (((1,), (1,)), ((), ())), preferred_element_type=jnp.float32)


def wait_bytes(ref, sem):
    pltpu.make_async_copy(ref, ref, sem).wait()


def step_kernel(
    experts,
    owner_h, grads_h, momentum_h, query_h, key_h, peaks_h, flags_h,
    new_momentum_h, returned_h, owned_h, query_out_h, key_out_h,
    owner_s, peaks_v, flags_v, query_v, key_v, query_o, key_o,
    grads_v, momentum_v, staged, new_v, x_own, x_pair, x_next, u_own,
    gram, poly, gram_next,
    part0, part1, part2, part3, part4, far0, far1, far2, far3, far4,
    peak_y, peak_z, peak_s, gamma_v, root_v,
    load_sem, store_sem, in_send, in_recv, pair_send, pair_recv,
    far_send, far_recv, share_send, share_recv, out_send, out_recv,
    peak_send, peak_recv,
):
    parts = (part0, part1, part2, part3, part4)
    fars = (far0, far1, far2, far3, far4)
    me = lax.axis_index("dp")
    y = lax.axis_index("expert")
    z = me // SEATS
    seat = lax.rem(me, SEATS)
    core = lax.rem(me, 2)
    group = me // 4
    width = grads_v.shape[2]
    quarter = width // 4
    pair = me + 1 - 2 * core
    across = me + 2 - 4 * lax.rem(me // 2, 2)

    def columns_of(part):
        return pl.ds(pl.multiple_of(part * quarter, LANES), quarter)

    my_columns = columns_of(lax.rem(me, 4))

    def remote(src, dst, send, recv, where):
        return pltpu.make_async_remote_copy(
            src_ref=src, dst_ref=dst, send_sem=send, recv_sem=recv,
            device_id=where, device_id_type=MESH,
        )

    loads = [
        pltpu.make_async_copy(src, dst, load_sem.at[n])
        for n, (src, dst) in enumerate(
            (
                (owner_h, owner_s),
                (grads_h, grads_v),
                (momentum_h, momentum_v),
                (peaks_h, peaks_v),
                (flags_h, flags_v),
                (query_h, query_v),
                (key_h, key_v),
            )
        )
    ]
    for load in loads:
        load.start()

    barrier = pltpu.get_barrier_semaphore()

    def greet(i, carry):
        pl.semaphore_signal(
            barrier, inc=1, device_id={"dp": lax.rem(me + i, DEVICES)}, device_id_type=MESH
        )
        return carry

    lax.fori_loop(1, DEVICES, greet, 0)

    def greet_expert(i, carry):
        pl.semaphore_signal(
            barrier, inc=1, device_id={"expert": lax.rem(y + i, experts)}, device_id_type=MESH
        )
        return carry

    lax.fori_loop(1, experts, greet_expert, 0)

    for load in loads[:4]:
        load.wait()
    peak_y[y] = jnp.zeros((8, LANES), jnp.float32)
    peak_y[y, :, 0:HEADS] = jnp.broadcast_to(peaks_v[...], (8, HEADS))

    def momentum_of(k):
        return (
            MOMENTUM_DECAY * momentum_v[k].astype(jnp.float32) + grads_v[k].astype(jnp.float32)
        ).astype(jnp.bfloat16)

    def stage(g, carry):
        k = jnp.int32(0)
        for m in range(MATS):
            k = jnp.where(owner_s[0, m] == g, m, k)
        staged[g] = momentum_of(k)
        return carry

    lax.fori_loop(0, MATS, stage, 0)
    pl.semaphore_wait(barrier, DEVICES - 1 + experts - 1)

    def send_peak_y(i, carry):
        remote(
            peak_y.at[y], peak_y.at[y], peak_send.at[0], peak_recv.at[0],
            {"expert": lax.rem(y + i, experts)},
        ).start()
        return carry

    lax.fori_loop(1, experts, send_peak_y, 0)

    def send_window(n):
        their_z = wrapped(z - OFFSETS[n])
        dst = x_own.at[pl.ds(pl.multiple_of(n * PLANE_ROWS + seat * ROWS, ROWS), ROWS)]
        arrival = in_recv.at[[n in slots for slots in STEP_SLOTS].index(True)]

        def send_rows(i, carry):
            there = their_z * SEATS + lax.rem(seat + i, SEATS)
            src = staged.at[there // 4, :, columns_of(lax.rem(there, 4))]

            @pl.when(there != me)
            def _():
                remote(src, dst, in_send.at[n], arrival, {"dp": there}).start()

            @pl.when(there == me)
            def _():
                pltpu.make_async_copy(src, dst, arrival).start()

            return carry

        lax.fori_loop(0, SEATS, send_rows, 0)

    def wait_window(n):
        sent = PLANE_ROWS - (ROWS if OFFSETS[n] == 0 else 0)
        wait_bytes(x_own.at[pl.ds(0, sent)], in_send.at[n])

    def send_next(first, last):
        for n in range(first, last):
            wait_window(n - LOOK)
            send_window(n)

    for n in range(LOOK):
        send_window(n)

    def new_momentum_step(k, carry):
        new_v[k] = momentum_of(k)
        return carry

    lax.fori_loop(0, MATS, new_momentum_step, 0)
    store_momentum = pltpu.make_async_copy(new_v, new_momentum_h, store_sem.at[0])
    store_momentum.start()

    wait_bytes(peak_y.at[pl.ds(0, experts - 1)], peak_recv.at[0])
    peak_z[z] = jnp.max(peak_y[...], axis=0)

    def send_peak_z(i, carry):
        remote(
            peak_z.at[z], peak_z.at[z], peak_send.at[1], peak_recv.at[1],
            {"dp": lax.rem(z + i, PLANES) * SEATS + seat},
        ).start()
        return carry

    lax.fori_loop(1, PLANES, send_peak_z, 0)

    def rows_of(i):
        return pl.ds(i * BLOCK, BLOCK)

    pair_copies = []
    far_copies = []
    share_copies = []

    def spot_of(s):
        first, count, columns = step_extent(s)
        rows, lanes = part_shape(s)
        if rows == count:
            return pl.ds(first, count), pl.ds(pl.multiple_of(core * lanes, LANES), lanes)
        return pl.ds(pl.multiple_of(first + core * rows, ROWS), rows), pl.ds(0, columns)

    def partial_gram(s):
        first, count, columns = step_extent(s)
        if part_shape(s)[0] == count:
            left, right = pl.ds(first, count), spot_of(s)[1]
        else:
            left, right = spot_of(s)[0], pl.ds(0, columns)
        return dot_nt(x_own[left, :], x_own[right, :]) + dot_nt(x_pair[left, :], x_pair[right, :])

    def share(s):
        far_copies[s].wait_recv()
        spot = spot_of(s)
        gram[spot] = (
            parts[s][...].astype(jnp.float32) + fars[s][...].astype(jnp.float32)
        ).astype(jnp.bfloat16)
        copy = remote(
            gram.at[spot], gram.at[spot], share_send.at[s], share_recv.at[s], {"dp": pair}
        )
        copy.start()
        share_copies.append(copy)

    def mirror(s):
        share_copies[s].wait_recv()
        first, count, _ = step_extent(s)
        if first:
            gram[0:first, first : first + count] = gram[first : first + count, 0:first].T

    for s in range(STEPS):
        send_next(
            min(PLANES, STEP_SLOTS[s][0] + LOOK), min(PLANES, STEP_SLOTS[s][-1] + 1 + LOOK)
        )
        first, count, _ = step_extent(s)
        arrived = pl.ds(first, count)
        wait_bytes(x_own.at[arrived], in_recv.at[s])
        copy = remote(
            x_own.at[arrived], x_pair.at[arrived], pair_send.at[s], pair_recv.at[s], {"dp": pair}
        )
        copy.start()
        pair_copies.append(copy)
        copy.wait_recv()
        parts[s][...] = partial_gram(s).astype(jnp.bfloat16)
        copy = remote(parts[s], fars[s], far_send.at[s], far_recv.at[s], {"dp": across})
        copy.start()
        far_copies.append(copy)
        if s > 0:
            share(s - 1)
        if s > 1:
            mirror(s - 2)
    mirror(STEPS - 2)
    share(STEPS - 1)
    mirror(STEPS - 1)

    diagonal = gram[rows_of(0), rows_of(0)].astype(jnp.float32)
    for i in range(1, BLOCKS):
        diagonal = diagonal + gram[rows_of(i), rows_of(i)].astype(jnp.float32)
    down = lax.broadcasted_iota(jnp.int32, (BLOCK, BLOCK), 0)
    along = lax.broadcasted_iota(jnp.int32, (BLOCK, BLOCK), 1)
    squares = jnp.sum(jnp.where(down == along, diagonal, 0.0), axis=0, keepdims=True)
    squares = jnp.sum(squares, axis=1, keepdims=True)
    scale = lax.rsqrt(squares + EPSILON)
    scale2 = 1.0 / (squares + EPSILON)

    for i in range(BLOCKS):
        rows = rows_of(i)
        poly[rows, :] = (
            (COEF_B * scale2) * gram[rows, :].astype(jnp.float32)
            + (COEF_C * scale2 * scale2) * dot_nn(gram[rows, :], gram[...])
        ).astype(jnp.bfloat16)

    for i in range(BLOCKS):
        rows = rows_of(i)
        x_next[rows, :] = (
            scale
            * (COEF_A * x_own[rows, :].astype(jnp.float32) + dot_nn(poly[rows, :], x_own[...]))
        ).astype(jnp.bfloat16)

    for i in range(BLOCKS):
        rows = rows_of(i)
        left = scale2 * (
            COEF_A * gram[rows, :].astype(jnp.float32) + dot_nn(poly[rows, :], gram[...])
        )
        gram_next[rows, :] = (
            COEF_A * left + dot_nn(left.astype(jnp.bfloat16), poly[...])
        ).astype(jnp.bfloat16)

    wait_bytes(peak_z.at[pl.ds(0, PLANES - 1)], peak_recv.at[1])
    peak_s[seat] = jnp.max(peak_z[...], axis=0)

    def send_peak_s(i, carry):
        remote(
            peak_s.at[seat], peak_s.at[seat], peak_send.at[2], peak_recv.at[2],
            {"dp": z * SEATS + lax.rem(seat + i, SEATS)},
        ).start()
        return carry

    lax.fori_loop(1, SEATS, send_peak_s, 0)

    def send_update(slot):
        plane = wrapped(z + OFFSETS[slot])
        first = slot * PLANE_ROWS

        def send_rows(i, carry):
            their_seat = lax.rem(seat + i, SEATS)
            there = plane * SEATS + their_seat
            src = u_own.at[pl.ds(pl.multiple_of(first + their_seat * ROWS, ROWS), ROWS)]
            dst = returned_h.at[group, :, my_columns]

            @pl.when(there != me)
            def _():
                remote(src, dst, out_send, out_recv, {"dp": there}).start()

            @pl.when(there == me)
            def _():
                pltpu.make_async_copy(src, dst, out_recv).start()

            return carry

        lax.fori_loop(0, SEATS, send_rows, 0)
        spot = owned_h.at[0, 0, pl.ds(pl.multiple_of(plane * PLANE_ROWS, ROWS), PLANE_ROWS)]
        pltpu.make_async_copy(
            u_own.at[pl.ds(first, PLANE_ROWS)], spot, store_sem.at[1]
        ).start()

    for i in range(BLOCKS):
        rows = rows_of(i)
        own = gram_next[rows, :]
        term = (
            COEF_B * own.astype(jnp.float32) + COEF_C * dot_nn(own, gram_next[...])
        ).astype(jnp.bfloat16)
        last = (
            COEF_A * x_next[rows, :].astype(jnp.float32) + dot_nn(term, x_next[...])
        ).astype(jnp.bfloat16)
        u_own[rows, :] = (last.astype(jnp.float32) * math.sqrt(width)).astype(jnp.bfloat16)
        send_update(2 * i)
        send_update(2 * i + 1)

    for load in loads[4:]:
        load.wait()
    wait_bytes(peak_s.at[pl.ds(0, SEATS - 1)], peak_recv.at[2])
    top = jnp.max(peak_s[...], axis=0)
    head_down = lax.broadcasted_iota(jnp.int32, (HEADS, HEADS), 0)
    head_along = lax.broadcasted_iota(jnp.int32, (HEADS, HEADS), 1)
    same = head_down == head_along
    peak = jnp.max(
        jnp.where(same, jnp.broadcast_to(top[0:1, 0:HEADS], (HEADS, HEADS)), 0.0),
        axis=1, keepdims=True,
    )
    flag = jnp.max(
        jnp.where(
            same, jnp.broadcast_to(flags_v[...].astype(jnp.float32), (HEADS, HEADS)), 0.0
        ),
        axis=1, keepdims=True,
    )
    peak = jnp.broadcast_to(peak, (HEADS, LANES))
    flag = jnp.broadcast_to(flag, (HEADS, LANES))
    gamma = jnp.where(flag == 1.0, jnp.minimum(1.0, CLIP_TAU / peak), 1.0)
    gamma_v[...] = gamma
    root_v[...] = jnp.sqrt(gamma)
    low = lax.broadcasted_iota(jnp.int32, (1, LANES), 1) < LANES // 2

    def clip_step(j, carry):
        root0 = root_v[pl.ds(2 * j, 1), :]
        root1 = root_v[pl.ds(2 * j + 1, 1), :]
        gamma0 = gamma_v[pl.ds(2 * j, 1), :]
        gamma1 = gamma_v[pl.ds(2 * j + 1, 1), :]
        scales = (root0, jnp.where(low, gamma0, root1), jnp.where(low, root1, gamma1))
        for n, factor in enumerate(scales):
            lanes = pl.ds(pl.multiple_of((3 * j + n) * LANES, LANES), LANES)
            query_o[:, lanes] = (query_v[:, lanes].astype(jnp.float32) * factor).astype(
                jnp.bfloat16
            )
        for n, factor in enumerate((root0, root1)):
            lanes = pl.ds(pl.multiple_of((2 * j + n) * LANES, LANES), LANES)
            key_o[:, lanes] = (key_v[:, lanes].astype(jnp.float32) * factor).astype(jnp.bfloat16)
        return carry

    lax.fori_loop(0, HEADS // 2, clip_step, 0)
    store_query = pltpu.make_async_copy(query_o, query_out_h, store_sem.at[2])
    store_key = pltpu.make_async_copy(key_o, key_out_h, store_sem.at[3])
    store_query.start()
    store_key.start()

    store_momentum.wait()
    store_query.wait()
    store_key.wait()
    wait_bytes(peak_y.at[pl.ds(0, experts - 1)], peak_send.at[0])
    wait_bytes(peak_z.at[pl.ds(0, PLANES - 1)], peak_send.at[1])
    wait_bytes(peak_s.at[pl.ds(0, SEATS - 1)], peak_send.at[2])
    for copy in pair_copies + far_copies + share_copies:
        copy.wait_send()
    for n in range(PLANES - LOOK, PLANES):
        wait_window(n)
    wait_bytes(u_own.at[pl.ds(0, HID - ROWS)], out_send)
    wait_bytes(u_own, store_sem.at[1])

    wait_bytes(returned_h, out_recv)


def finish_kernel(
    owner_h, new_momentum_i, returned_i, owned_i, query_i, key_i,
    new_momentum_h, update_h, owned_h, query_h, key_h,
    owner_s, new_momentum_v, update_v, owned_v, query_v, key_v,
    owner_sem, load_sem, store_sem, pick_sem, put_sem,
):
    load_owner = pltpu.make_async_copy(owner_h, owner_s, owner_sem)
    load_owner.start()
    plain = (
        (new_momentum_i, new_momentum_v, new_momentum_h),
        (owned_i, owned_v, owned_h),
        (query_i, query_v, query_h),
        (key_i, key_v, key_h),
    )
    loads = [
        pltpu.make_async_copy(src, mid, load_sem.at[n]) for n, (src, mid, _) in enumerate(plain)
    ]
    stores = [
        pltpu.make_async_copy(mid, dst, store_sem.at[n]) for n, (_, mid, dst) in enumerate(plain)
    ]
    for load in loads:
        load.start()
    load_owner.wait()
    picks = [
        pltpu.make_async_copy(returned_i.at[owner_s[0, k]], update_v.at[k], pick_sem.at[k])
        for k in range(MATS)
    ]
    puts = [
        pltpu.make_async_copy(update_v.at[k], update_h.at[k], put_sem.at[k]) for k in range(MATS)
    ]
    for pick in picks:
        pick.start()
    for load, store in zip(loads, stores):
        load.wait()
        store.start()
    for pick, put in zip(picks, puts):
        pick.wait()
        put.start()
    for copy in stores + puts:
        copy.wait()


def shards(experts, grads, momentum, owner, query_weight, key_weight, head_maxima, clip_flags):
    mats, rows, width = grads.shape
    quarter = width // 4
    anywhere = pl.BlockSpec(memory_space=pl.ANY)
    bf16 = jnp.bfloat16
    shard = jax.ShapeDtypeStruct((mats, rows, width), bf16)
    block = pltpu.VMEM((mats, rows, width), bf16)
    half = pltpu.VMEM((HID, quarter), bf16)
    square = pltpu.VMEM((HID, HID), bf16)
    lanes = [pltpu.VMEM(part_shape(s), bf16) for s in range(STEPS)]
    dma = pltpu.SemaphoreType.DMA
    results = (
        shard,
        shard,
        jax.ShapeDtypeStruct((1, 1, HID, quarter), bf16),
        jax.ShapeDtypeStruct(query_weight.shape, bf16),
        jax.ShapeDtypeStruct(key_weight.shape, bf16),
    )
    parts = pl.pallas_call(
        functools.partial(step_kernel, experts),
        out_shape=results,
        in_specs=[anywhere] * 7,
        out_specs=(anywhere,) * 5,
        scratch_shapes=[
            pltpu.SMEM((1, mats), jnp.int32),
            pltpu.VMEM((1, HEADS), jnp.float32),
            pltpu.VMEM((1, HEADS), jnp.int32),
            pltpu.VMEM(query_weight.shape, bf16),
            pltpu.VMEM(key_weight.shape, bf16),
            pltpu.VMEM(query_weight.shape, bf16),
            pltpu.VMEM(key_weight.shape, bf16),
            block, block, block, block, half, half, half, half, square, square, square,
            *lanes, *lanes,
            pltpu.VMEM((experts, 8, LANES), jnp.float32),
            pltpu.VMEM((PLANES, 8, LANES), jnp.float32),
            pltpu.VMEM((SEATS, 8, LANES), jnp.float32),
            pltpu.VMEM((HEADS, LANES), jnp.float32),
            pltpu.VMEM((HEADS, LANES), jnp.float32),
            dma((7,)), dma((4,)), dma((PLANES,)), dma((STEPS,)), dma((STEPS,)), dma((STEPS,)),
            dma((STEPS,)), dma((STEPS,)), dma((STEPS,)), dma((STEPS,)), dma, dma,
            dma((3,)), dma((3,)),
        ],
        compiler_params=pltpu.CompilerParams(
            collective_id=0, has_side_effects=True, vmem_limit_bytes=60 * 1024 * 1024
        ),
        name="muon_step",
    )(
        owner, grads, momentum, query_weight, key_weight, head_maxima,
        clip_flags.reshape(1, HEADS),
    )
    return pl.pallas_call(
        finish_kernel,
        out_shape=results,
        in_specs=[anywhere] * 6,
        out_specs=(anywhere,) * 5,
        scratch_shapes=[
            pltpu.SMEM((1, mats), jnp.int32),
            *[pltpu.VMEM(result.shape, bf16) for result in results],
            dma, dma((4,)), dma((4,)), dma((MATS,)), dma((MATS,)),
        ],
        compiler_params=pltpu.CompilerParams(vmem_limit_bytes=60 * 1024 * 1024),
        name="finish",
    )(owner, *parts)


def solution(mesh):
    in_specs = (
        P("expert", "dp", None),
        P("expert", "dp", None),
        P("expert", None),
        P("dp", None),
        P("dp", None),
        P(("dp", "expert"), None),
        P(),
    )
    out_specs = (
        P("expert", "dp", None),
        P("expert", "dp", None),
        P("expert", "dp", None, None),
        P("dp", None),
        P("dp", None),
    )
    return jax.shard_map(
        functools.partial(shards, mesh.shape["expert"]),
        mesh=mesh, in_specs=in_specs, out_specs=out_specs, check_vma=False,
    )
```

time: 193 us -> 127 us (0.66)
  Pallas kernels: 182 us -> 126 us
  local copies, waits for them, and re-layouts: 10 us -> 0 us
    pallas_call x2, Pallas kernels: 182 us -> 126 us  [the longest x1 121 us: shards(): pl.pallas_call(functools.partial(step_kernel, experts), out_shape=results...]
    unnamed x18 -> x0, local copies, waits for them, and re-layouts: 10 us -> none
where the time goes in v2:
time: 127 us
  Pallas kernels  126 us (99%)
    pallas_call x1, Pallas kernels, shards(): pl.pallas_call(functools.partial(step_kernel, experts), out_shape=results...  121 us
    pallas_call x1, Pallas kernels, shards(): pl.pallas_call(finish_kernel, out_shape=results, in_specs=[anywhere] * 6,...  4.78 us

profile of v2, /device:TPU:25, one launch (start us, length us, event | category | flops | bytes accessed | tf_op | source)
XLA Modules:
  0.0 126.9 jit_solution(5667534939771370223)
XLA Ops:
  0.6 121.3 %muon_step.1 = (bf16[16,16,3584]{2,1,0:T(8,128)(2,1)}, bf16[16,16,3584]{2,1,0:T(8,128)(2,1)}, bf16[1,1,1024,896]{3,2,1,0:T(8,128)(2,1)}, bf16[24,12288]{1,0:T(8,128)(2,1)}, bf16[8,8192]{1,0:T(8,128)(2,1)}) custom-call(s32[1,16]{1,0:T(1,128)} %owner_h.3, bf16[16,16,3584]{2,1,0:T(8,128)(2,1)} %grads_h.1, bf16[16,16,3584]{2,1,0:T(8,128)(2,1)} %momentum_h.1, ...), custom_call_target="tpu_custom_call" | custom-call | tf_op jit(solution)/shard_map/muon_step/pallas_call | solution.py:492
  121.9 4.8 %finish.1 = (bf16[16,16,3584]{2,1,0:T(8,128)(2,1)}, bf16[16,16,3584]{2,1,0:T(8,128)(2,1)}, bf16[1,1,1024,896]{3,2,1,0:T(8,128)(2,1)}, bf16[24,12288]{1,0:T(8,128)(2,1)}, bf16[8,8192]{1,0:T(8,128)(2,1)}) custom-call(s32[1,16]{1,0:T(1,128)} %owner_h.3, bf16[16,16,3584]{2,1,0:T(8,128)(2,1)} %get-tuple-element.10.new_momentum_i, ...), custom_call_target="tpu_custom_call" | custom-call | tf_op jit(solution)/shard_map/finish/pallas_call | solution.py:524

commit v3 on v2

--- a/solution.py
+++ b/solution.py
@@ -31,7 +31,7 @@
 LANES = 128
 
 OFFSETS = (3, -3, 2, -2, 1, -1, 0, 4)
-LOOK = 2
+LOOK = 8
 STEP_SLOTS = ((0, 1), (2, 3), (4, 5), (6,), (7,))
 STEPS = len(STEP_SLOTS)
 BLOCKS = HID // BLOCK
@@ -70,11 +70,12 @@
     new_momentum_h, returned_h, owned_h, query_out_h, key_out_h,
     owner_s, peaks_v, flags_v, query_v, key_v, query_o, key_o,
     grads_v, momentum_v, staged, new_v, x_own, x_pair, x_next, u_own,
-    gram, poly, gram_next,
+    gram, poly, gram_next, left_v,
     part0, part1, part2, part3, part4, far0, far1, far2, far3, far4,
     peak_y, peak_z, peak_s, gamma_v, root_v,
     load_sem, store_sem, in_send, in_recv, pair_send, pair_recv,
-    far_send, far_recv, share_send, share_recv, out_send, out_recv,
+    far_send, far_recv, share_send, share_recv, poly_send, poly_recv, next_send, next_recv,
+    out_send, out_recv,
     peak_send, peak_recv,
 ):
     parts = (part0, part1, part2, part3, part4)
@@ -153,7 +154,6 @@
         staged[g] = momentum_of(k)
         return carry
 
-    lax.fori_loop(0, MATS, stage, 0)
     pl.semaphore_wait(barrier, DEVICES - 1 + experts - 1)
 
     def send_peak_y(i, carry):
@@ -167,6 +167,7 @@
 
     def send_window(n):
         their_z = wrapped(z - OFFSETS[n])
+        lax.fori_loop(2 * their_z, 2 * their_z + 2, stage, 0)
         dst = x_own.at[pl.ds(pl.multiple_of(n * PLANE_ROWS + seat * ROWS, ROWS), ROWS)]
         arrival = in_recv.at[[n in slots for slots in STEP_SLOTS].index(True)]
 
@@ -258,7 +259,7 @@
         if first:
             gram[0:first, first : first + count] = gram[first : first + count, 0:first].T
 
-    for s in range(STEPS):
+    def arrive(s):
         send_next(
             min(PLANES, STEP_SLOTS[s][0] + LOOK), min(PLANES, STEP_SLOTS[s][-1] + 1 + LOOK)
         )
@@ -270,7 +271,12 @@
         )
         copy.start()
         pair_copies.append(copy)
-        copy.wait_recv()
+
+    arrive(0)
+    for s in range(STEPS):
+        if s + 1 < STEPS:
+            arrive(s + 1)
+        pair_copies[s].wait_recv()
         parts[s][...] = partial_gram(s).astype(jnp.bfloat16)
         copy = remote(parts[s], fars[s], far_send.at[s], far_recv.at[s], {"dp": across})
         copy.start()
@@ -293,28 +299,53 @@
     scale = lax.rsqrt(squares + EPSILON)
     scale2 = 1.0 / (squares + EPSILON)
 
-    for i in range(BLOCKS):
-        rows = rows_of(i)
+    def half_rows(which, i):
+        return pl.ds(pl.multiple_of(which * (HID // 2) + i * BLOCK, BLOCK), BLOCK)
+
+    half_blocks = BLOCKS // 2
+    poly_copies = []
+    next_copies = []
+    for i in range(half_blocks):
+        rows = half_rows(core, i)
         poly[rows, :] = (
             (COEF_B * scale2) * gram[rows, :].astype(jnp.float32)
             + (COEF_C * scale2 * scale2) * dot_nn(gram[rows, :], gram[...])
         ).astype(jnp.bfloat16)
-
-    for i in range(BLOCKS):
-        rows = rows_of(i)
+        copy = remote(
+            poly.at[rows], poly.at[rows], poly_send.at[i], poly_recv.at[i], {"dp": pair}
+        )
+        copy.start()
+        poly_copies.append(copy)
+
+    def iterate_rows(rows):
         x_next[rows, :] = (
             scale
             * (COEF_A * x_own[rows, :].astype(jnp.float32) + dot_nn(poly[rows, :], x_own[...]))
         ).astype(jnp.bfloat16)
 
-    for i in range(BLOCKS):
-        rows = rows_of(i)
-        left = scale2 * (
+    for i in range(half_blocks):
+        iterate_rows(half_rows(core, i))
+
+    for i in range(half_blocks):
+        rows = half_rows(core, i)
+        left_v[i] = scale2 * (
             COEF_A * gram[rows, :].astype(jnp.float32) + dot_nn(poly[rows, :], gram[...])
         )
+    for copy in poly_copies:
+        copy.wait_recv()
+    for i in range(half_blocks):
+        rows = half_rows(core, i)
+        left = left_v[i]
         gram_next[rows, :] = (
             COEF_A * left + dot_nn(left.astype(jnp.bfloat16), poly[...])
         ).astype(jnp.bfloat16)
+        copy = remote(
+            gram_next.at[rows], gram_next.at[rows], next_send.at[i], next_recv.at[i], {"dp": pair}
+        )
+        copy.start()
+        next_copies.append(copy)
+    for i in range(half_blocks):
+        iterate_rows(half_rows(1 - core, i))
 
     wait_bytes(peak_z.at[pl.ds(0, PLANES - 1)], peak_recv.at[1])
     peak_s[seat] = jnp.max(peak_z[...], axis=0)
@@ -354,6 +385,8 @@
             u_own.at[pl.ds(first, PLANE_ROWS)], spot, store_sem.at[1]
         ).start()
 
+    for copy in next_copies:
+        copy.wait_recv()
     for i in range(BLOCKS):
         rows = rows_of(i)
         own = gram_next[rows, :]
@@ -419,7 +452,7 @@
     wait_bytes(peak_y.at[pl.ds(0, experts - 1)], peak_send.at[0])
     wait_bytes(peak_z.at[pl.ds(0, PLANES - 1)], peak_send.at[1])
     wait_bytes(peak_s.at[pl.ds(0, SEATS - 1)], peak_send.at[2])
-    for copy in pair_copies + far_copies + share_copies:
+    for copy in pair_copies + far_copies + share_copies + poly_copies + next_copies:
         copy.wait_send()
     for n in range(PLANES - LOOK, PLANES):
         wait_window(n)
@@ -432,7 +465,7 @@
 def finish_kernel(
     owner_h, new_momentum_i, returned_i, owned_i, query_i, key_i,
     new_momentum_h, update_h, owned_h, query_h, key_h,
-    owner_s, new_momentum_v, update_v, owned_v, query_v, key_v,
+    owner_s, new_momentum_v, returned_v, owned_v, query_v, key_v,
     owner_sem, load_sem, store_sem, pick_sem, put_sem,
 ):
     load_owner = pltpu.make_async_copy(owner_h, owner_s, owner_sem)
@@ -451,21 +484,18 @@
     ]
     for load in loads:
         load.start()
-    load_owner.wait()
-    picks = [
-        pltpu.make_async_copy(returned_i.at[owner_s[0, k]], update_v.at[k], pick_sem.at[k])
-        for k in range(MATS)
-    ]
-    puts = [
-        pltpu.make_async_copy(update_v.at[k], update_h.at[k], put_sem.at[k]) for k in range(MATS)
-    ]
-    for pick in picks:
-        pick.start()
+    load_returned = pltpu.make_async_copy(returned_i, returned_v, pick_sem)
+    load_returned.start()
     for load, store in zip(loads, stores):
         load.wait()
         store.start()
-    for pick, put in zip(picks, puts):
-        pick.wait()
+    load_owner.wait()
+    load_returned.wait()
+    puts = [
+        pltpu.make_async_copy(returned_v.at[owner_s[0, k]], update_h.at[k], put_sem.at[k])
+        for k in range(MATS)
+    ]
+    for put in puts:
         put.start()
     for copy in stores + puts:
         copy.wait()
@@ -503,6 +533,7 @@
             pltpu.VMEM(query_weight.shape, bf16),
             pltpu.VMEM(key_weight.shape, bf16),
             block, block, block, block, half, half, half, half, square, square, square,
+            pltpu.VMEM((BLOCKS // 2, BLOCK, HID), jnp.float32),
             *lanes, *lanes,
             pltpu.VMEM((experts, 8, LANES), jnp.float32),
             pltpu.VMEM((PLANES, 8, LANES), jnp.float32),
@@ -510,7 +541,8 @@
             pltpu.VMEM((HEADS, LANES), jnp.float32),
             pltpu.VMEM((HEADS, LANES), jnp.float32),
             dma((7,)), dma((4,)), dma((PLANES,)), dma((STEPS,)), dma((STEPS,)), dma((STEPS,)),
-            dma((STEPS,)), dma((STEPS,)), dma((STEPS,)), dma((STEPS,)), dma, dma,
+            dma((STEPS,)), dma((STEPS,)), dma((STEPS,)), dma((STEPS,)),
+            *[dma((BLOCKS // 2,))] * 4, dma, dma,
             dma((3,)), dma((3,)),
         ],
         compiler_params=pltpu.CompilerParams(
@@ -529,7 +561,7 @@
         scratch_shapes=[
             pltpu.SMEM((1, mats), jnp.int32),
             *[pltpu.VMEM(result.shape, bf16) for result in results],
-            dma, dma((4,)), dma((4,)), dma((MATS,)), dma((MATS,)),
+            dma, dma((4,)), dma((4,)), dma, dma((MATS,)),
         ],
         compiler_params=pltpu.CompilerParams(vmem_limit_bytes=60 * 1024 * 1024),
         name="finish",

time: 127 us -> 123 us (0.969)
  Pallas kernels: 126 us -> 122 us
    pallas_call x1, Pallas kernels: 121 us -> 117 us  [shards(): pl.pallas_call(functools.partial(step_kernel, experts), out_shape=results...]
where the time goes in v3:
time: 123 us; the launch traced here: 122 us
  Pallas kernels  122 us (99%)
    pallas_call x1, Pallas kernels, shards(): pl.pallas_call(functools.partial(step_kernel, experts), out_shape=results...  117 us
    pallas_call x1, Pallas kernels, shards(): pl.pallas_call(finish_kernel, out_shape=results, in_specs=[anywhere] * 6,...  5.09 us

profile of v3, /device:TPU:25, one launch (start us, length us, event | category | flops | bytes accessed | tf_op | source)
XLA Modules:
  0.0 122.4 jit_solution(12080571575896924529)
XLA Ops:
  0.6 116.7 %muon_step.1 = (bf16[16,16,3584]{2,1,0:T(8,128)(2,1)}, bf16[16,16,3584]{2,1,0:T(8,128)(2,1)}, bf16[1,1,1024,896]{3,2,1,0:T(8,128)(2,1)}, bf16[24,12288]{1,0:T(8,128)(2,1)}, bf16[8,8192]{1,0:T(8,128)(2,1)}) custom-call(s32[1,16]{1,0:T(1,128)} %owner_h.3, bf16[16,16,3584]{2,1,0:T(8,128)(2,1)} %grads_h.1, bf16[16,16,3584]{2,1,0:T(8,128)(2,1)} %momentum_h.1, ...), custom_call_target="tpu_custom_call" | custom-call | tf_op jit(solution)/shard_map/muon_step/pallas_call | solution.py:522
  117.3 5.1 %finish.1 = (bf16[16,16,3584]{2,1,0:T(8,128)(2,1)}, bf16[16,16,3584]{2,1,0:T(8,128)(2,1)}, bf16[1,1,1024,896]{3,2,1,0:T(8,128)(2,1)}, bf16[24,12288]{1,0:T(8,128)(2,1)}, bf16[8,8192]{1,0:T(8,128)(2,1)}) custom-call(s32[1,16]{1,0:T(1,128)} %owner_h.3, bf16[16,16,3584]{2,1,0:T(8,128)(2,1)} %get-tuple-element.10.new_momentum_i, ...), custom_call_target="tpu_custom_call" | custom-call | tf_op jit(solution)/shard_map/finish/pallas_call | solution.py:556

commit v4 on v3

--- a/solution.py
+++ b/solution.py
@@ -32,7 +32,8 @@
 
 OFFSETS = (3, -3, 2, -2, 1, -1, 0, 4)
 LOOK = 8
-STEP_SLOTS = ((0, 1), (2, 3), (4, 5), (6,), (7,))
+LAG = 3
+STEP_SLOTS = tuple((n,) for n in range(PLANES))
 STEPS = len(STEP_SLOTS)
 BLOCKS = HID // BLOCK
 
@@ -71,15 +72,16 @@
     owner_s, peaks_v, flags_v, query_v, key_v, query_o, key_o,
     grads_v, momentum_v, staged, new_v, x_own, x_pair, x_next, u_own,
     gram, poly, gram_next, left_v,
-    part0, part1, part2, part3, part4, far0, far1, far2, far3, far4,
+    part0, part1, part2, part3, part4, part5, part6, part7,
+    far0, far1, far2, far3, far4, far5, far6, far7,
     peak_y, peak_z, peak_s, gamma_v, root_v,
     load_sem, store_sem, in_send, in_recv, pair_send, pair_recv,
     far_send, far_recv, share_send, share_recv, poly_send, poly_recv, next_send, next_recv,
     out_send, out_recv,
     peak_send, peak_recv,
 ):
-    parts = (part0, part1, part2, part3, part4)
-    fars = (far0, far1, far2, far3, far4)
+    parts = (part0, part1, part2, part3, part4, part5, part6, part7)
+    fars = (far0, far1, far2, far3, far4, far5, far6, far7)
     me = lax.axis_index("dp")
     y = lax.axis_index("expert")
     z = me // SEATS
@@ -281,12 +283,13 @@
         copy = remote(parts[s], fars[s], far_send.at[s], far_recv.at[s], {"dp": across})
         copy.start()
         far_copies.append(copy)
-        if s > 0:
-            share(s - 1)
-        if s > 1:
-            mirror(s - 2)
-    mirror(STEPS - 2)
-    share(STEPS - 1)
+        if s >= LAG:
+            share(s - LAG)
+        if s > LAG:
+            mirror(s - LAG - 1)
+    for s in range(STEPS - LAG, STEPS):
+        share(s)
+        mirror(s - 1)
     mirror(STEPS - 1)
 
     diagonal = gram[rows_of(0), rows_of(0)].astype(jnp.float32)
@@ -387,8 +390,8 @@
 
     for copy in next_copies:
         copy.wait_recv()
-    for i in range(BLOCKS):
-        rows = rows_of(i)
+    for slots in ((0,), (1,), (2, 3), (4, 5), (6, 7)):
+        rows = pl.ds(slots[0] * PLANE_ROWS, len(slots) * PLANE_ROWS)
         own = gram_next[rows, :]
         term = (
             COEF_B * own.astype(jnp.float32) + COEF_C * dot_nn(own, gram_next[...])
@@ -397,8 +400,8 @@
             COEF_A * x_next[rows, :].astype(jnp.float32) + dot_nn(term, x_next[...])
         ).astype(jnp.bfloat16)
         u_own[rows, :] = (last.astype(jnp.float32) * math.sqrt(width)).astype(jnp.bfloat16)
-        send_update(2 * i)
-        send_update(2 * i + 1)
+        for slot in slots:
+            send_update(slot)
 
     for load in loads[4:]:
         load.wait()

time: 123 us -> 122 us (level)
  the two profiles are of different devices: /device:TPU:25 before, /device:TPU:33 now
where the time goes in v4:
time: 122 us
  Pallas kernels  121 us (99%)
    pallas_call x1, Pallas kernels, shards(): pl.pallas_call(functools.partial(step_kernel, experts), out_shape=results...  116 us
    pallas_call x1, Pallas kernels, shards(): pl.pallas_call(finish_kernel, out_shape=results, in_specs=[anywhere] * 6,...  5.09 us

profile of v4, /device:TPU:33, one launch (start us, length us, event | category | flops | bytes accessed | tf_op | source)
XLA Modules:
  0.0 121.9 jit_solution(6225837624954076523)
XLA Ops:
  0.6 116.0 %muon_step.1 = (bf16[16,16,3584]{2,1,0:T(8,128)(2,1)}, bf16[16,16,3584]{2,1,0:T(8,128)(2,1)}, bf16[1,1,1024,896]{3,2,1,0:T(8,128)(2,1)}, bf16[24,12288]{1,0:T(8,128)(2,1)}, bf16[8,8192]{1,0:T(8,128)(2,1)}) custom-call(s32[1,16]{1,0:T(1,128)} %owner_h.3, bf16[16,16,3584]{2,1,0:T(8,128)(2,1)} %grads_h.1, bf16[16,16,3584]{2,1,0:T(8,128)(2,1)} %momentum_h.1, ...), custom_call_target="tpu_custom_call" | custom-call | tf_op jit(solution)/shard_map/muon_step/pallas_call | solution.py:525
  116.7 5.1 %finish.1 = (bf16[16,16,3584]{2,1,0:T(8,128)(2,1)}, bf16[16,16,3584]{2,1,0:T(8,128)(2,1)}, bf16[1,1,1024,896]{3,2,1,0:T(8,128)(2,1)}, bf16[24,12288]{1,0:T(8,128)(2,1)}, bf16[8,8192]{1,0:T(8,128)(2,1)}) custom-call(s32[1,16]{1,0:T(1,128)} %owner_h.3, bf16[16,16,3584]{2,1,0:T(8,128)(2,1)} %get-tuple-element.10.new_momentum_i, ...), custom_call_target="tpu_custom_call" | custom-call | tf_op jit(solution)/shard_map/finish/pallas_call | solution.py:559
